TPU v7x, 256 devices: a whole 4x4x8 slice. The times are simulated.
256 devices in a mesh: row: 8 (over y_hi, x), cent: 32 (over y_lo, z, core).
Axes of the slice: x: 4, y: 4 (y_hi: 2, y_lo: 2; y = y_hi * 2 + y_lo), z: 8, core: 2. Of those that a mesh axis runs over, the one named last changes fastest.
Arguments:
- embeddings: bfloat16 [65536, 1024], P('row', 'cent'), may hold values from -6 to 6
- assigned: int32 [65536], P('row'), may hold values from 0 to 8191
- centroids: bfloat16 [8192, 1024], P('cent'), may hold values from -0.1875 to 0.1875
Outputs:
- new_centroids: bfloat16 [8192, 1024], P('cent')
- best_cosine: float32 [65536], P('row')
All inputs are finite; a program needn't handle non-finite values.
Results may differ from a plain program's by a relative error of at most 0.015.
Values may be sent and summed in bfloat16 or wider, within the bound.
A program may use at most 128 MiB of HBM per device.

v0:
```python
import jax
import jax.numpy as jnp
from jax import lax
from jax.sharding import PartitionSpec as P


def normalize_rows(values):
    return values * lax.rsqrt(jnp.sum(values * values, axis=1, keepdims=True) + 1e-06)


def onehot_sums(unit, ids, total_rows):
    rows_here = unit.shape[0]
    width = unit.shape[1]
    step_rows = min(512, rows_here)
    count = rows_here // step_rows
    unit_blocks = unit.reshape(count, step_rows, width)
    id_blocks = ids.reshape(count, step_rows)
    columns = jnp.arange(total_rows, dtype=jnp.int32)

    def add_block(total, pair):
        piece, block_ids = pair
        onehot = (block_ids[:, None] == columns[None, :]).astype(jnp.bfloat16)
        product = lax.dot_general(
            onehot, piece, (((0,), (0,)), ((), ())), preferred_element_type=jnp.float32
        )
        return (total + product, None)

    local_sum, _ = lax.scan(
        add_block, jnp.zeros((total_rows, width), jnp.float32), (unit_blocks, id_blocks)
    )
    return lax.optimization_barrier(local_sum.astype(jnp.bfloat16)).astype(jnp.float32)


def per_device(embeddings, assigned, centroids):
    owned = centroids.shape[0]
    full_rows = lax.all_gather(embeddings, "cent", axis=1, tiled=True)
    unit = normalize_rows(full_rows.astype(jnp.float32)).astype(jnp.bfloat16)
    local_ids = assigned - lax.axis_index("cent") * owned
    terms = onehot_sums(unit, local_ids, owned)
    sums = lax.psum(terms.astype(jnp.bfloat16), "row").astype(jnp.float32)
    new_centroids = normalize_rows(centroids.astype(jnp.float32) + sums).astype(jnp.bfloat16)
    rows_here = unit.shape[0]
    step_rows = min(512, rows_here)
    unit_blocks = unit.reshape(rows_here // step_rows, step_rows, unit.shape[1])

    def best_block(carry, piece):
        scores = lax.dot_general(
            piece, new_centroids, (((1,), (1,)), ((), ())), preferred_element_type=jnp.float32
        )
        return (carry, jnp.max(scores, axis=1))

    _, maxima = lax.scan(best_block, 0, unit_blocks)
    best_cosine = lax.pmax(maxima.reshape(rows_here).astype(jnp.bfloat16), "cent").astype(
        jnp.float32
    )
    return (new_centroids, best_cosine)


def solution(mesh):
    in_specs = (P("row", "cent"), P("row"), P("cent", None))
    out_specs = (P("cent", None), P("row"))
    return jax.shard_map(
        per_device, mesh=mesh, in_specs=in_specs, out_specs=out_specs, check_vma=False
    )
```

profile of v0, /device:TPU:1, one launch (start us, length us, event | category | flops | bytes accessed | tf_op | source)
XLA Modules:
  0.0 417.3 jit_solution(15785434237475762546)
XLA Ops:
  7.2 0.0 all-gather.2.cloned.1.call-start
  7.2 0.7 all-gather.2.cloned.1.call-update
  7.9 0.0 all-reduce.2.cloned.1.call-start
  8.0 0.8 broadcast_subtract_fusion
  8.7 105.1 %all-gather.2.cloned.1.call-done = bf16[8192,1024]{0,1:T(8,128)(2,1)} async-done(((bf16[8192,32]{0,1:T(8,128)(2,1)}), bf16[8192,1024]{0,1:T(8,128)(2,1)}) %all-gather.2.cloned.1.call-update) | async-done | bytes 16777232 | tf_op jit(solution)/shard_map/all_gather | solution.py:36
  113.9 0.0 copy-start
  113.9 7.4 %fusion.9 = f32[8192]{0:T(1024)S(1)} fusion(bf16[8192,1024]{0,1:T(8,128)(2,1)} %all-gather.2.cloned.1.call-done), kind=kLoop, calls=%fused_computation.14 | loop fusion | flops 25157632 | bytes 16809984 | tf_op jit(solution)/shard_map/reduce_sum | solution.py:8
  121.3 3.3 copy-done
  124.6 8.3 %fusion.10 = bf16[8192,1024]{0,1:T(8,128)(2,1)} fusion(bf16[8192,1024]{0,1:T(8,128)(2,1)S(1)} %copy-done, f32[8192]{0:T(1024)S(1)} %add_rsqrt_fusion), kind=kLoop, calls=%fused_computation.15 | loop fusion | flops 25165824 | bytes 33587200 | tf_op jit(solution)/shard_map/convert_element_type | solution.py:37
  132.9 22.4 %copy.5 = bf16[8192,1024]{1,0:T(8,128)(2,1)} copy(bf16[8192,1024]{0,1:T(8,128)(2,1)} %fusion.10) | data formatting | bytes 33554432 | tf_op jit(solution)/shard_map/convert_element_type | solution.py:37
  155.4 0.0 copy-start.1
  155.4 31.1 %while.22 = (s32[]{:T(128)}, f32[256,1024]{1,0:T(8,128)S(1)}, s32[16,512]{1,0:T(8,128)S(1)}, bf16[16,512,1024]{2,1,0:T(8,128)(2,1)}, s32[]{:T(128)}, /*index=5*/s32[]{:T(128)}) while((s32[]{:T(128)}, f32[256,1024]{1,0:T(8,128)S(1)}, s32[16,512]{1,0:T(8,128)S(1)}, bf16[16,512,1024]{2,1,0:T(8,128)(2,1)}, s32[]{:T(128)}, ...), condition=%wide.region_2.3_spmd.clone, body=%wide.region_1.2_spmd.clone.sunk | while | flops 269090816 | bytes 3152467 | solution.py:28
  155.4 2.0 convolution_add_fusion.2
  157.4 1.9 convolution_add_fusion.2
  159.3 1.9 convolution_add_fusion.2
  161.3 1.9 convolution_add_fusion.2
  163.2 1.9 convolution_add_fusion.2
  165.1 1.9 convolution_add_fusion.2
  167.1 1.9 convolution_add_fusion.2
  169.0 1.9 convolution_add_fusion.2
  171.0 1.9 convolution_add_fusion.2
  172.9 1.9 convolution_add_fusion.2
  174.9 1.9 convolution_add_fusion.2
  176.8 1.9 convolution_add_fusion.2
  178.8 1.9 convolution_add_fusion.2
  180.7 1.9 convolution_add_fusion.2
  182.6 1.9 convolution_add_fusion.2
  184.6 1.9 convolution_add_fusion.2
  186.5 0.9 convert_element_type.33
  187.4 0.0 all-reduce.2.cloned.1.call-update
  187.4 85.1 %all-reduce.2.cloned.1.call-done = bf16[256,1024]{1,0:T(8,128)(2,1)} async-done(((bf16[256,1024]{1,0:T(8,128)(2,1)}), bf16[256,1024]{1,0:T(8,128)(2,1)}) %all-reduce.2.cloned.1.call-update) | async-done | bytes 524304 | tf_op jit(solution)/shard_map/psum | solution.py:40
  272.6 0.0 copy-done.1
  272.6 1.3 multiply_reduce_fusion
  273.9 1.2 multiply_convert_fusion
  275.1 28.6 %while.21 = (s32[]{:T(128)}, bf16[16,512]{1,0:T(8,128)(2,1)S(1)}, bf16[16,512,1024]{2,1,0:T(8,128)(2,1)}, bf16[256,1024]{1,0:T(8,128)(2,1)S(1)}, s32[]{:T(128)}, /*index=5*/s32[]{:T(128)}) while((s32[]{:T(128)}, bf16[16,512]{1,0:T(8,128)(2,1)S(1)}, bf16[16,512,1024]{2,1,0:T(8,128)(2,1)}, bf16[256,1024]{1,0:T(8,128)(2,1)S(1)}, s32[]{:T(128)}, ...), condition=%wide.region_7.8_spmd, body=%wide.region_5.7_spmd.sunk | while | flops 268566016 | bytes 1579593 | solution.py:52
  275.1 1.7 convolution_reduce_fusion.2
  276.9 1.7 convolution_reduce_fusion.2
  278.7 1.7 convolution_reduce_fusion.2
  280.4 1.7 convolution_reduce_fusion.2
  282.2 1.7 convolution_reduce_fusion.2
  284.0 1.7 convolution_reduce_fusion.2
  285.8 1.7 convolution_reduce_fusion.2
  287.6 1.7 convolution_reduce_fusion.2
  289.4 1.7 convolution_reduce_fusion.2
  291.2 1.7 convolution_reduce_fusion.2
  292.9 1.7 convolution_reduce_fusion.2
  294.7 1.7 convolution_reduce_fusion.2
  296.5 1.7 convolution_reduce_fusion.2
  298.3 1.7 convolution_reduce_fusion.2
  300.1 1.7 convolution_reduce_fusion.2
  301.9 1.7 convolution_reduce_fusion.2
  303.7 0.0 copy-start.2
  303.7 106.2 %pmax.7 = bf16[8192]{0:T(1024)(128)(2,1)S(1)} all-reduce(bf16[8192]{0:T(1024)(128)(2,1)S(1)} %bitcast.26), channel_id=1, replica_groups=mesh['row'=8,'cent'=32] {'cent'}, use_global_device_ids=true, to_apply=%region_8.9 | all-reduce | flops 8192 | bytes 32768 | tf_op jit(solution)/shard_map/pmax | solution.py:53
  409.8 0.6 convert_element_type.38
  410.5 0.0 copy-done.2
  (38 shorter events, 0.9 us)
Async XLA Ops:
  7.2 106.7 %all-gather.2.cloned.1.call-start = ((), (), s32[]{:S(2)}) async-start(), calls=%async_computation | async-start | bytes 17301504 | tf_op jit(solution)/shard_map/all_gather | solution.py:36
  7.9 264.7 %all-reduce.2.cloned.1.call-start = ((), (), s32[]{:S(2)}) async-start(), calls=%async_computation.1 | async-start | bytes 1048576 | tf_op jit(solution)/shard_map/psum | solution.py:40
  113.9 10.7 %copy-start = (bf16[8192,1024]{0,1:T(8,128)(2,1)S(1)}, bf16[8192,1024]{0,1:T(8,128)(2,1)}, u32[]{:S(2)}) copy-start(bf16[8192,1024]{0,1:T(8,128)(2,1)} %all-gather.2.cloned.1.call-done) | copy-start | bytes 50331652
  155.4 117.2 %copy-start.1 = (bf16[256,1024]{1,0:T(8,128)(2,1)S(1)}, bf16[256,1024]{1,0:T(8,128)(2,1)}, u32[]{:S(2)}) copy-start(bf16[256,1024]{1,0:T(8,128)(2,1)} %param.9) | copy-start | bytes 1572868
  303.7 106.8 %copy-start.2 = (bf16[256,1024]{1,0:T(8,128)(2,1)}, bf16[256,1024]{1,0:T(8,128)(2,1)S(1)}, u32[]{:S(2)}) copy-start(bf16[256,1024]{1,0:T(8,128)(2,1)S(1)} %get-tuple-element.181) | copy-start | bytes 1572868
Sparse Core Ops, SparseCore 0:
  9.9 103.9 all-gather.1
  187.5 84.9 all-reduce.1
where the time goes:
time: 422 us; the launch traced here: 417 us
  waiting for transfers between devices  191 us (45%)
  blocking collectives  106 us (25%)
  matrix products  57.9 us (14%)
  local copies, waits for them, and re-layouts  26.6 us (6%)
  other arithmetic  20.5 us (5%)
  between operations  14.1 us (3%)
    pmax x1, blocking collectives, per_device(): lax.pmax(maxima.reshape(rows_here).astype(jnp.bfloat16), 'cent')  106 us
    all_gather x1, waiting for transfers between devices, per_device(): full_rows = lax.all_gather(embeddings, 'cent', axis=1, tiled=True)  105 us
    psum x1, waiting for transfers between devices, per_device(): sums = lax.psum(terms.astype(jnp.bfloat16), 'row').astype(jnp.float32)  85.1 us
    dot_general x16, matrix products, add_block(): lax.dot_general(onehot, piece, (((0,), (0,)), ((), ())), preferred_elemen...  30.4 us
    dot_general x16, matrix products, best_block(): lax.dot_general(piece, new_centroids, (((1,), (1,)), ((), ())), preferred...  27.5 us
    convert_element_type x1, local copies, waits for them, and re-layouts, per_device(): unit = normalize_rows(full_rows.astype(jnp.float32)).astype(jnp.bfloat16)  22.4 us
    reduce_sum x2, other arithmetic, normalize_rows(): jnp.sum(values * values, axis=1, keepdims=True) + 1e-06  8.69 us
  transfers between devices with their start and end apart: 2, of which 2 were waited for; matrix products, arithmetic and copies ran while one was open for 0% of the time, Pallas kernels for 0%

commit v1 on v0

v1 whole, which is shorter than its diff:
```python
import functools

import jax
import jax.numpy as jnp
from jax import lax
from jax.experimental import pallas as pl
from jax.experimental.pallas import tpu as pltpu
from jax.sharding import PartitionSpec as P

MESH = pl.DeviceIdType.MESH
F = 32
EPS = 1e-06


def kernel(nr, nz, x_ref, id_ref, cent_ref, nc_out, best_out,
           q, qr, myinv, inv, e, kr, acc, part, got, summed, turned, centbuf, ncs, top, tops,
           loc_sem, n_send, n_recv, i_send, i_recv, ez_send, ef_send, e_recv, c_send, c_recv,
           p_send, p_recv, s_send, s_recv, g_send, g_recv, t_send, t_recv):
    nc = 4 * nz
    rows = x_ref.shape[1]
    own_rows = rows // nc
    a_count = nz // 2
    tile_rows = rows // a_count
    j_count = 256 // nz
    r = lax.axis_index("row")
    c = lax.axis_index("cent")
    core = lax.rem(c, 2)
    z = lax.rem(c // 2, nz)
    y = c // (2 * nz)
    a = z // 2

    def cent_id(yy, zz, cc):
        return yy * (2 * nz) + zz * 2 + cc

    def remote(src, dst, send, recv, row, cent):
        return pltpu.make_async_remote_copy(
            src_ref=src, dst_ref=dst, send_sem=send, recv_sem=recv,
            device_id=(row, cent), device_id_type=MESH)

    def drain(ref, sem):
        pltpu.make_async_copy(ref, ref, sem).wait()

    def span(start, size):
        return pl.ds(pl.multiple_of(start, size), size)

    barrier = pltpu.get_barrier_semaphore()

    @pl.loop(1, nc)
    def _(i):
        pl.semaphore_signal(barrier, inc=1, device_id=(r, lax.rem(c + i, nc)), device_id_type=MESH)

    @pl.loop(1, nr)
    def _(i):
        pl.semaphore_signal(barrier, inc=1, device_id=(lax.rem(r + i, nr), c), device_id_type=MESH)

    step = min(1024, rows)

    @pl.loop(0, rows // step)
    def _(t):
        here = span(t * step, step)
        wide = x_ref[:, here].astype(jnp.float32)
        q[:, here] = jnp.sum(wide * wide, axis=0, keepdims=True)

    pl.semaphore_wait(barrier, nc - 1 + nr - 1)

    @pl.loop(1, nc)
    def _(i):
        d = lax.rem(c + i, nc)
        remote(q.at[:, span(d * own_rows, own_rows)], qr.at[c], n_send, n_recv, r, d).start()

    own = pltpu.make_async_copy(q.at[:, span(c * own_rows, own_rows)], qr.at[c], loc_sem.at[0])
    own.start()
    own_e = pltpu.make_async_copy(x_ref.at[:, span(a * tile_rows, tile_rows)], e.at[c], loc_sem.at[1])
    own_e.start()
    own_c = pltpu.make_async_copy(cent_ref.at[span(r * j_count, j_count), :], centbuf.at[a], loc_sem.at[2])
    own_c.start()
    own.wait()
    drain(qr.at[pl.ds(0, nc - 1)], n_recv)
    myinv[...] = lax.rsqrt(jnp.sum(qr[...], axis=0) + EPS)

    @pl.loop(1, nc)
    def _(i):
        d = lax.rem(c + i, nc)
        remote(myinv, inv.at[:, span(c * own_rows, own_rows)], i_send, i_recv, r, d).start()

    own_i = pltpu.make_async_copy(myinv, inv.at[:, span(c * own_rows, own_rows)], loc_sem.at[3])
    own_i.start()

    @pl.loop(1, nz)
    def _(i):
        zz = lax.rem(z + i, nz)
        d = cent_id(y, zz, core)
        remote(x_ref.at[:, span((zz // 2) * tile_rows, tile_rows)], e.at[c], ez_send, e_recv.at[c], r, d).start()

    @pl.loop(1, a_count)
    def _(i):
        d = cent_id(y, lax.rem(z + 2 * i, nz), core)
        remote(cent_ref.at[span(r * j_count, j_count), :], centbuf.at[a], c_send, c_recv, r, d).start()

    y_mate = cent_id(1 - y, z, core)
    core_mate = cent_id(y, z, 1 - core)

    def pass_on(piece, to_y):
        if to_y:
            remote(e.at[piece], e.at[piece], ef_send, e_recv.at[piece], r, y_mate).start()
        remote(e.at[piece], e.at[piece], ef_send, e_recv.at[piece], r, core_mate).start()

    def pass_z(i):
        half = (i + 1) // 2
        turn = half * (2 * lax.rem(i, 2) - 1) + nz
        piece = cent_id(y, lax.rem(z + turn, nz), core)
        drain(e.at[piece], e_recv.at[piece])
        pass_on(piece, True)

    def pass_y(i):
        piece = cent_id(1 - y, lax.rem(z + i, nz), core)
        drain(e.at[piece], e_recv.at[piece])
        pass_on(piece, False)

    own_e.wait()
    pass_on(c, True)

    own_i.wait()
    drain(inv.at[:, pl.ds(0, rows - own_rows)], i_recv)

    acc[...] = jnp.zeros_like(acc)
    klo_count = 4 * nr
    shift_c = nr * j_count

    @pl.loop(0, rows // step)
    def _(t):
        here = span(t * step, step)
        ids = id_ref[:, here]
        unit = (x_ref[:, here].astype(jnp.float32) * inv[:, here]).astype(jnp.bfloat16)
        cc = ids // shift_c
        rr = lax.rem(ids, shift_c) // j_count
        jj = lax.rem(ids, j_count)
        zz = lax.rem(cc // 2, nz)
        lane = lax.rem(cc, 2) * 128 + (zz // 2) * j_count + jj
        low = rr * 4 + (cc // (2 * nz)) * 2 + lax.rem(zz, 2)
        lane_b = jnp.broadcast_to(lane.astype(jnp.float32), (256, step)).astype(jnp.bfloat16)
        iota = lax.broadcasted_iota(jnp.int32, (256, step), 0).astype(jnp.float32).astype(jnp.bfloat16)
        one = jnp.bfloat16(1)
        nil = jnp.bfloat16(0)
        hot = jnp.where(lane_b == iota, one, nil)
        low_b = jnp.broadcast_to(low.astype(jnp.float32), (F, step)).astype(jnp.bfloat16)
        for j in range(klo_count):
            kr[j * F:(j + 1) * F, :] = jnp.where(low_b == jnp.bfloat16(j), unit, nil)
        acc[...] += lax.dot_general(kr[...], hot, (((1,), (1,)), ((), ())), preferred_element_type=jnp.float32)

    part[...] = acc[...].astype(jnp.bfloat16)

    @pl.loop(1, nr)
    def _(i):
        rr = lax.rem(r + i, nr)
        remote(part.at[span(rr * 128, 128), :], got.at[r], p_send, p_recv, rr, c).start()

    own_p = pltpu.make_async_copy(part.at[span(r * 128, 128), :], got.at[r], loc_sem.at[4])
    own_p.start()

    @pl.loop(1, nz // 2 + 1)
    def _(i):
        pass_z(i)

    own_p.wait()
    drain(got.at[pl.ds(0, nr - 1)], p_recv)
    total = got[0].astype(jnp.float32)
    for i in range(1, nr):
        total = total + got[i].astype(jnp.float32)
    summed[...] = total.astype(jnp.bfloat16)

    @pl.loop(1, nc)
    def _(i):
        d = lax.rem(c + i, nc)
        u = (d // (2 * nz)) * 2 + lax.rem(d // 2, 2)
        remote(summed.at[span(u * F, F), span(lax.rem(d, 2) * 128, 128)], turned.at[span(c * F, F), :],
               s_send, s_recv, r, d).start()

    u_own = y * 2 + lax.rem(z, 2)
    own_s = pltpu.make_async_copy(summed.at[span(u_own * F, F), span(core * 128, 128)],
                                  turned.at[span(c * F, F), :], loc_sem.at[5])
    own_s.start()
    own_c.wait()
    if a_count > 1:
        drain(centbuf.at[pl.ds(0, a_count - 1)], c_recv)
    old = centbuf[...].reshape(128, cent_ref.shape[1]).astype(jnp.float32)
    own_s.wait()
    drain(turned.at[pl.ds(0, (nc - 1) * F), :], s_recv)
    fresh = turned[...].astype(jnp.float32).T + old
    fresh = fresh * lax.rsqrt(jnp.sum(fresh * fresh, axis=1, keepdims=True) + EPS)
    ncs[r] = fresh.astype(jnp.bfloat16)

    @pl.loop(1, nr)
    def _(i):
        rr = lax.rem(r + i, nr)
        remote(ncs.at[r], ncs.at[r], g_send, g_recv, rr, c).start()

    @pl.loop(nz // 2 + 1, nz)
    def _(i):
        pass_z(i)

    @pl.loop(0, nz)
    def _(i):
        pass_y(i)

    @pl.loop(0, 2 * nz)
    def _(i):
        piece = cent_id(i // nz, lax.rem(i, nz), 1 - core)
        drain(e.at[piece], e_recv.at[piece])

    drain(ncs.at[pl.ds(0, nr - 1)], g_recv)
    for i in range(nr):
        nc_out[i * j_count:(i + 1) * j_count, :] = ncs[i, span(a * j_count, j_count), :]

    width = nc * F
    wide_rows = 256
    every = ncs[...].reshape(nr * 128, width)

    @pl.loop(0, tile_rows // wide_rows)
    def _(t):
        here = span(t * wide_rows, wide_rows)
        scores = jnp.dot(every, e[:, :, here].reshape(width, wide_rows), preferred_element_type=jnp.float32)
        top[:, here] = jnp.max(scores, axis=0, keepdims=True)

    @pl.loop(1, nc)
    def _(i):
        remote(top, tops.at[c], t_send, t_recv, r, lax.rem(c + i, nc)).start()

    own_t = pltpu.make_async_copy(top, tops.at[c], loc_sem.at[6])
    own_t.start()
    drain(qr.at[pl.ds(0, nc - 1)], n_send)
    drain(inv.at[:, pl.ds(0, rows - own_rows)], i_send)
    drain(e.at[pl.ds(0, nz - 1)], ez_send)
    drain(e.at[pl.ds(0, 3 * nz)], ef_send)
    if a_count > 1:
        drain(centbuf.at[pl.ds(0, a_count - 1)], c_send)
    drain(got.at[pl.ds(0, nr - 1)], p_send)
    drain(turned.at[pl.ds(0, (nc - 1) * F), :], s_send)
    drain(ncs.at[pl.ds(0, nr - 1)], g_send)
    own_t.wait()
    drain(tops.at[pl.ds(0, nc - 1)], t_recv)
    for aa in range(a_count):
        best = tops[4 * aa]
        for yy in range(2):
            for k in range(4):
                best = jnp.maximum(best, tops[yy * 2 * nz + 4 * aa + k])
        here = pl.ds(aa * tile_rows, tile_rows)
        best_out[:, here] = best * inv[:, here]
    drain(tops.at[pl.ds(0, nc - 1)], t_send)


def per_device(nr, nz, embeddings, assigned, centroids):
    nc = 4 * nz
    rows = embeddings.shape[0]
    owned, width = centroids.shape
    a_count = nz // 2
    tile_rows = rows // a_count
    j_count = 256 // nz
    own_rows = rows // nc
    step = min(1024, rows)
    bf, fl = jnp.bfloat16, jnp.float32
    dma = pltpu.SemaphoreType.DMA
    vmem = pl.BlockSpec(memory_space=pltpu.VMEM)
    out, best = pl.pallas_call(
        functools.partial(kernel, nr, nz),
        out_shape=(jax.ShapeDtypeStruct((owned, width), bf), jax.ShapeDtypeStruct((1, rows), fl)),
        in_specs=[vmem] * 3,
        out_specs=(vmem, vmem),
        scratch_shapes=[
            pltpu.VMEM((1, rows), fl),
            pltpu.VMEM((nc, 1, own_rows), fl),
            pltpu.VMEM((1, own_rows), fl),
            pltpu.VMEM((1, rows), fl),
            pltpu.VMEM((nc, F, tile_rows), bf),
            pltpu.VMEM((4 * nr * F, step), bf),
            pltpu.VMEM((4 * nr * F, 256), fl),
            pltpu.VMEM((4 * nr * F, 256), bf),
            pltpu.VMEM((nr, 128, 256), bf),
            pltpu.VMEM((128, 256), bf),
            pltpu.VMEM((width, 128), bf),
            pltpu.VMEM((a_count, j_count, width), bf),
            pltpu.VMEM((nr, 128, width), bf),
            pltpu.VMEM((1, tile_rows), fl),
            pltpu.VMEM((nc, 1, tile_rows), fl),
            dma((8,)), dma, dma, dma, dma, dma, dma, dma((nc,)), dma, dma,
            dma, dma, dma, dma, dma, dma, dma, dma,
        ],
        compiler_params=pltpu.CompilerParams(
            collective_id=0, has_side_effects=True, vmem_limit_bytes=48 * 1024 * 1024),
    )(embeddings.T, assigned.reshape(1, rows), centroids)
    return out, best.reshape(rows)


def solution(mesh):
    nr, nz = mesh.shape["row"], mesh.shape["cent"] // 4
    return jax.shard_map(
        functools.partial(per_device, nr, nz),
        mesh=mesh,
        in_specs=(P("row", "cent"), P("row"), P("cent", None)),
        out_specs=(P("cent", None), P("row")),
        check_vma=False,
    )
```

time: 422 us -> 111 us (0.26); the launches traced: 417 us -> 111 us
  waiting for transfers between devices: 191 us -> 0 us
  Pallas kernels: 0 us -> 106 us
  blocking collectives: 106 us -> 0 us
  matrix products: 57.9 us -> 0 us
  local copies, waits for them, and re-layouts: 26.6 us -> 4.25 us
  other arithmetic: 20.5 us -> 0 us
  between operations: 14.1 us -> 0.65 us
    pmax x1 -> x0, blocking collectives: 106 us -> none  [per_device(): lax.pmax(maxima.reshape(rows_here).astype(jnp.bfloat16), 'cent')]
    pallas_call x0 -> x1, Pallas kernels: none -> 106 us  [per_device(): pl.pallas_call(functools.partial(kernel, nr, nz), out_shape=(jax.ShapeDty...]
    all_gather x1 -> x0, waiting for transfers between devices: 105 us -> none  [per_device(): full_rows = lax.all_gather(embeddings, 'cent', axis=1, tiled=True)]
    psum x1 -> x0, waiting for transfers between devices: 85.1 us -> none  [per_device(): sums = lax.psum(terms.astype(jnp.bfloat16), 'row').astype(jnp.float32)]
    dot_general x32 -> x0, matrix products: 57.9 us -> none  [the longest x16 30.4 us: add_block(): lax.dot_general(onehot, piece, (((0,), (0,)), ((), ())), preferred_elemen...]
    convert_element_type x1 -> x0, local copies, waits for them, and re-layouts: 22.4 us -> none  [per_device(): unit = normalize_rows(full_rows.astype(jnp.float32)).astype(jnp.bfloat16)]
    convert_element_type x4 -> x0, other arithmetic: 11.1 us -> none  [the longest x1 8.34 us: per_device(): unit = normalize_rows(full_rows.astype(jnp.float32)).astype(jnp.bfloat16)]
    reduce_sum x2 -> x0, other arithmetic: 8.69 us -> none  [normalize_rows(): jnp.sum(values * values, axis=1, keepdims=True) + 1e-06]
  transfers between devices with their start and end apart: 2 -> 0, of which waited for: 2 -> 0; matrix products, arithmetic and copies ran while one was open for 0% -> 0% of each run, Pallas kernels for 0% -> 0%
where the time goes in v1:
time: 111 us
  Pallas kernels  106 us (95%)
  local copies, waits for them, and re-layouts  4.25 us (4%)
    pallas_call x1, Pallas kernels, per_device(): pl.pallas_call(functools.partial(kernel, nr, nz), out_shape=(jax.ShapeDty...  106 us
    unnamed x8, local copies, waits for them, and re-layouts  4.25 us

profile of v1, /device:TPU:1, one launch (start us, length us, event | category | flops | bytes accessed | tf_op | source)
XLA Modules:
  0.0 111.0 jit_solution(16986827673024410089)
XLA Ops:
  0.6 0.0 copy-start
  0.6 1.0 copy-done
  1.7 0.0 copy-start.1
  1.7 1.0 copy-done.1
  2.7 0.0 copy-start.2
  2.7 0.8 copy-done.2
  3.5 106.1 %shard_map.50 = (bf16[256,1024]{1,0:T(8,128)(2,1)S(1)}, f32[1,8192]{1,0:T(1,128)S(1)}) custom-call(bf16[32,8192]{1,0:T(8,128)(2,1)S(1)} %bitcast.3, s32[1,8192]{1,0:T(1,128)S(1)} %bitcast.4, bf16[256,1024]{1,0:T(8,128)(2,1)S(1)} %copy-done.1), custom_call_target="tpu_custom_call" | custom-call | tf_op jit(solution)/shard_map/pallas_call | solution.py:264
  109.6 0.8 copy.7
  110.4 0.6 copy.8
Async XLA Ops:
  0.6 1.0 copy-start
  1.7 1.0 copy-start.1
  2.7 0.8 copy-start.2

commit v2 on v1

v2 whole, which is shorter than its diff:
```python
import functools

import jax
import jax.numpy as jnp
from jax import lax
from jax.experimental import pallas as pl
from jax.experimental.pallas import tpu as pltpu
from jax.sharding import PartitionSpec as P

MESH = pl.DeviceIdType.MESH
F = 32
EPS = 1e-06
CUT = 48


def kernel(nx, nz, x_hbm, id_ref, cent_hbm, nc_out, best_out,
           x_ref, q, qmate, qchip, inv, lanes, lows, e, kr, acc, part, got, summed, zb, turned, centbuf, ncs,
           top, topmate, tops, loc, m_send, m_recv, n_send, n_recv, ez_send, ef_send, e_recv, c_send, c_recv,
           p_send, p_recv, s_send, s_recv, g_send, ga_recv, gb_recv, t_send, t_recv):
    nr = 2 * nx
    nc = 4 * nz
    chips = 2 * nz
    rows = x_ref.shape[1]
    lines = rows // 128
    half = lines // 2
    a_count = nz // 2
    tile_rows = rows // a_count
    tile_lines = tile_rows // 128
    j_count = 256 // nz
    width = nc * F
    r = lax.axis_index("row")
    c = lax.axis_index("cent")
    core = lax.rem(c, 2)
    z = lax.rem(c // 2, nz)
    y = c // (2 * nz)
    chip = c // 2
    a = z // 2
    x = lax.rem(r, nx)
    yh = r // nx

    def cent_id(yy, zz, cc):
        return yy * (2 * nz) + zz * 2 + cc

    core_mate = cent_id(y, z, 1 - core)
    y_mate = cent_id(1 - y, z, core)

    def remote(src, dst, send, recv, row, cent):
        return pltpu.make_async_remote_copy(
            src_ref=src, dst_ref=dst, send_sem=send, recv_sem=recv,
            device_id=(row, cent), device_id_type=MESH)

    def drain(ref, sem):
        pltpu.make_async_copy(ref, ref, sem).wait()

    def span(start, size):
        return pl.ds(pl.multiple_of(start, size), size)

    in_x = pltpu.make_async_copy(x_hbm, x_ref, loc.at[0])
    in_x.start()
    own_c = pltpu.make_async_copy(cent_hbm.at[span(r * j_count, j_count), :], centbuf.at[a], loc.at[1])
    own_c.start()
    barrier = pltpu.get_barrier_semaphore()
    pl.semaphore_signal(barrier, inc=1, device_id=(r, core_mate), device_id_type=MESH)

    @pl.loop(1, chips)
    def _(i):
        d = lax.rem(chip + i, chips) * 2 + core
        pl.semaphore_signal(barrier, inc=1, device_id=(r, d), device_id_type=MESH)

    @pl.loop(1, nr)
    def _(i):
        pl.semaphore_signal(barrier, inc=1, device_id=(lax.rem(r + i, nr), c), device_id_type=MESH)

    ids = id_ref[...]
    cc = ids // (nr * j_count)
    zz = lax.rem(cc // 2, nz)
    lanes[...] = (lax.rem(cc, 2) * 128 + (zz // 2) * j_count + lax.rem(ids, j_count)).astype(jnp.float32)
    lows[...] = (lax.rem(ids, nr * j_count) // j_count * 4 + (cc // (2 * nz)) * 2 + lax.rem(zz, 2)).astype(jnp.float32)

    in_x.wait()

    @pl.loop(0, lines // 8)
    def _(t):
        wide = x_ref[:, span(t * 1024, 1024)].astype(jnp.float32)
        squares = jnp.sum(wide * wide, axis=0, keepdims=True)
        q[span(t * 8, 8), :] = jnp.concatenate([squares[:, k * 128:(k + 1) * 128] for k in range(8)], axis=0)

    pl.semaphore_wait(barrier, 1 + chips - 1 + nr - 1)

    swap_q = remote(q.at[span((1 - core) * half, half), :], qmate, m_send.at[0], m_recv.at[0], r, core_mate)
    swap_q.start()
    own_e = pltpu.make_async_copy(x_ref.at[:, span(a * tile_rows, tile_rows)], e.at[c], loc.at[2])
    own_e.start()
    swap_q.wait()
    qchip[chip] = (q[span(core * half, half), :] + qmate[...]).astype(jnp.bfloat16)

    @pl.loop(1, chips)
    def _(i):
        d = lax.rem(chip + i, chips) * 2 + core
        remote(qchip.at[chip], qchip.at[chip], n_send, n_recv, r, d).start()

    def turned_z(i):
        return lax.rem(z + (i + 1) // 2 * (2 * lax.rem(i, 2) - 1) + nz, nz)

    @pl.loop(1, nz)
    def _(i):
        zz = turned_z(i)
        remote(x_ref.at[:, span((zz // 2) * tile_rows, tile_rows)], e.at[c], ez_send, e_recv.at[c],
               r, cent_id(y, zz, core)).start()

    own_c.wait()

    @pl.loop(1, a_count)
    def _(i):
        remote(centbuf.at[a], centbuf.at[a], c_send, c_recv, r, cent_id(y, lax.rem(z + 2 * i, nz), core)).start()

    def pass_on(piece, to_y):
        if to_y:
            remote(e.at[piece], e.at[piece], ef_send, e_recv.at[piece], r, y_mate).start()
        remote(e.at[piece], e.at[piece], ef_send, e_recv.at[piece], r, core_mate).start()

    def pass_z(i):
        piece = cent_id(y, turned_z(i), core)
        drain(e.at[piece], e_recv.at[piece])
        pass_on(piece, True)

    def pass_y(i):
        piece = cent_id(1 - y, lax.rem(z + i, nz), core)
        drain(e.at[piece], e_recv.at[piece])
        pass_on(piece, False)

    own_e.wait()
    pass_on(c, True)

    drain(qchip.at[pl.ds(0, chips - 1)], n_recv)
    squares = qchip[0].astype(jnp.float32)
    for i in range(1, chips):
        squares = squares + qchip[i].astype(jnp.float32)
    own_inv = inv.at[span(core * half, half), :]
    own_inv[...] = lax.rsqrt(squares + EPS)
    swap_i = remote(own_inv, own_inv, m_send.at[1], m_recv.at[1], r, core_mate)
    swap_i.start()
    swap_i.wait()

    acc[...] = jnp.zeros_like(acc)
    klo_count = 4 * nr

    def along(block):
        return jnp.concatenate([block[k:k + 1, :] for k in range(8)], axis=1)

    @pl.loop(0, lines // 8)
    def _(t):
        own8 = span(t * 8, 8)
        scale = along(inv[own8, :])
        unit = (x_ref[:, span(t * 1024, 1024)].astype(jnp.float32) * scale).astype(jnp.bfloat16)
        lane_b = jnp.broadcast_to(along(lanes[own8, :]), (256, 1024)).astype(jnp.bfloat16)
        iota = lax.broadcasted_iota(jnp.int32, (256, 1024), 0).astype(jnp.float32).astype(jnp.bfloat16)
        one = jnp.bfloat16(1)
        nil = jnp.bfloat16(0)
        hot = jnp.where(lane_b == iota, one, nil)
        low_b = jnp.broadcast_to(along(lows[own8, :]), (F, 1024)).astype(jnp.bfloat16)
        for j in range(klo_count):
            kr[j * F:(j + 1) * F, :] = jnp.where(low_b == jnp.bfloat16(j), unit, nil)
        acc[...] += lax.dot_general(kr[...], hot, (((1,), (1,)), ((), ())), preferred_element_type=jnp.float32)

    part[...] = acc[...].astype(jnp.bfloat16)

    @pl.loop(1, nr)
    def _(i):
        rr = lax.rem(r + i, nr)
        remote(part.at[span(rr * 128, 128), :], got.at[r], p_send, p_recv, rr, c).start()

    got[r] = part[span(r * 128, 128), :]

    first_pass = 3 * nz // 4 + 1

    @pl.loop(1, first_pass)
    def _(i):
        pass_z(i)

    drain(got.at[pl.ds(0, nr - 1)], p_recv)
    total = got[0].astype(jnp.float32)
    for i in range(1, nr):
        total = total + got[i].astype(jnp.float32)
    summed[...] = total.astype(jnp.bfloat16).reshape(4, F, 256)

    swap_s = remote(summed.at[:, :, span((1 - core) * 128, 128)], zb.at[:, span(core * F, F), :],
                    m_send.at[2], m_recv.at[2], r, core_mate)
    swap_s.start()
    zb[:, span(core * F, F), :] = summed[:, :, span(core * 128, 128)]
    swap_s.wait()

    @pl.loop(1, chips)
    def _(i):
        d = lax.rem(chip + i, chips)
        remote(zb.at[d // nz * 2 + lax.rem(d, 2)], turned.at[span(chip * 2 * F, 2 * F), :], s_send, s_recv,
               r, d * 2 + core).start()

    turned[span(chip * 2 * F, 2 * F), :] = zb[y * 2 + lax.rem(z, 2)]
    if a_count > 1:
        drain(centbuf.at[pl.ds(0, a_count - 1)], c_recv)

    @pl.loop(first_pass, nz)
    def _(i):
        pass_z(i)

    drain(turned.at[pl.ds(0, (chips - 1) * 2 * F), :], s_recv)
    fresh = turned[...].astype(jnp.float32).T + centbuf[...].reshape(128, width).astype(jnp.float32)
    fresh = fresh * lax.rsqrt(jnp.sum(fresh * fresh, axis=1, keepdims=True) + EPS)
    ncs[r] = fresh.astype(jnp.bfloat16)

    def pa(slot):
        return ncs.at[slot, pl.ds(0, CUT), :]

    def pb(slot):
        return ncs.at[slot, pl.ds(CUT, 128 - CUT), :]

    other = (1 - yh) * nx + x
    remote(pa(r), pa(r), g_send, ga_recv.at[r], other, c).start()
    for i in range(1, nx):
        mate = yh * nx + lax.rem(x + i, nx)
        remote(pb(r), pb(r), g_send, gb_recv.at[r], mate, c).start()
    for i in range(1, nx):
        mate = yh * nx + lax.rem(x + i, nx)
        remote(pa(r), pa(r), g_send, ga_recv.at[r], mate, c).start()
    remote(pb(r), pb(r), g_send, gb_recv.at[r], other, c).start()
    drain(pa(other), ga_recv.at[other])
    for i in range(1, nx):
        mate = yh * nx + lax.rem(x + i, nx)
        remote(pa(other), pa(other), g_send, ga_recv.at[other], mate, c).start()
    for i in range(1, nx):
        near = yh * nx + lax.rem(x + i, nx)
        drain(pb(near), gb_recv.at[near])
        remote(pb(near), pb(near), g_send, gb_recv.at[near], other, c).start()

    @pl.loop(0, nz)
    def _(i):
        pass_y(i)

    @pl.loop(0, 2 * nz)
    def _(i):
        piece = cent_id(i // nz, lax.rem(i, nz), 1 - core)
        drain(e.at[piece], e_recv.at[piece])

    for i in range(1, nx):
        near = yh * nx + lax.rem(x + i, nx)
        drain(pa(near), ga_recv.at[near])

    wide_rows = 256

    def score(first_slot, merge):
        block = ncs[pl.ds(first_slot, nx)].reshape(nx * 128, width)

        @pl.loop(0, tile_rows // wide_rows)
        def _(t):
            here = span(t * wide_rows, wide_rows)
            scores = jnp.dot(block, e[:, :, here].reshape(width, wide_rows), preferred_element_type=jnp.float32)
            best = jnp.max(scores, axis=0, keepdims=True)
            for k in range(2):
                line = pl.ds(t * 2 + k, 1)
                piece = best[:, k * 128:(k + 1) * 128]
                top[line, :] = jnp.maximum(top[line, :], piece) if merge else piece

    score(yh * nx, False)

    for i in range(1, nx):
        far = (1 - yh) * nx + lax.rem(x + i, nx)
        drain(pa(far), ga_recv.at[far])
        drain(pb(far), gb_recv.at[far])
    drain(pb(other), gb_recv.at[other])

    score((1 - yh) * nx, True)

    own_half = tile_lines // 2
    swap_t = remote(top.at[span((1 - core) * own_half, own_half), :], topmate, m_send.at[3], m_recv.at[3], r, core_mate)
    swap_t.start()
    for i in range(nr):
        nc_out[i * j_count:(i + 1) * j_count, :] = ncs[i, span(a * j_count, j_count), :]
    swap_t.wait()
    tops[chip] = jnp.maximum(top[span(core * own_half, own_half), :], topmate[...])

    @pl.loop(1, chips)
    def _(i):
        d = lax.rem(chip + i, chips) * 2 + core
        remote(tops.at[chip], tops.at[chip], t_send, t_recv, r, d).start()

    drain(qchip.at[pl.ds(0, chips - 1)], n_send)
    drain(e.at[pl.ds(0, nz - 1)], ez_send)
    drain(e.at[pl.ds(0, 3 * nz)], ef_send)
    if a_count > 1:
        drain(centbuf.at[pl.ds(0, a_count - 1)], c_send)
    drain(got.at[pl.ds(0, nr - 1)], p_send)
    drain(turned.at[pl.ds(0, (chips - 1) * 2 * F), :], s_send)
    drain(ncs.at[pl.ds(0, nr - 1)], g_send)

    drain(tops.at[pl.ds(0, chips - 1)], t_recv)
    for aa in range(a_count):
        best = tops[2 * aa]
        for yy in range(2):
            for k in range(2):
                best = jnp.maximum(best, tops[yy * nz + 2 * aa + k])
        first = aa * tile_lines
        here = span(first + core * own_half, own_half)
        best_out[here, :] = best * inv[here, :]
        there = best_out.at[here, :]
        remote(there, there, m_send.at[4], m_recv.at[4], r, core_mate).start()
    drain(best_out.at[pl.ds(0, half), :], m_recv.at[4])
    drain(best_out.at[pl.ds(0, half), :], m_send.at[4])
    drain(tops.at[pl.ds(0, chips - 1)], t_send)


def per_device(nx, nz, embeddings, assigned, centroids):
    nr, nc, chips = 2 * nx, 4 * nz, 2 * nz
    rows = embeddings.shape[0]
    owned, width = centroids.shape
    a_count = nz // 2
    tile_rows = rows // a_count
    lines = rows // 128
    j_count = 256 // nz
    bf, fl = jnp.bfloat16, jnp.float32
    dma = pltpu.SemaphoreType.DMA
    vmem = pl.BlockSpec(memory_space=pltpu.VMEM)
    hbm = pl.BlockSpec(memory_space=pltpu.HBM)
    out, best = pl.pallas_call(
        functools.partial(kernel, nx, nz),
        out_shape=(jax.ShapeDtypeStruct((owned, width), bf), jax.ShapeDtypeStruct((lines, 128), fl)),
        in_specs=[hbm, vmem, hbm],
        out_specs=(vmem, vmem),
        scratch_shapes=[
            pltpu.VMEM((F, rows), bf),
            pltpu.VMEM((lines, 128), fl),
            pltpu.VMEM((lines // 2, 128), fl),
            pltpu.VMEM((chips, lines // 2, 128), bf),
            pltpu.VMEM((lines, 128), fl),
            pltpu.VMEM((lines, 128), fl),
            pltpu.VMEM((lines, 128), fl),
            pltpu.VMEM((nc, F, tile_rows), bf),
            pltpu.VMEM((4 * nr * F, 1024), bf),
            pltpu.VMEM((4 * nr * F, 256), fl),
            pltpu.VMEM((4 * nr * F, 256), bf),
            pltpu.VMEM((nr, 128, 256), bf),
            pltpu.VMEM((4, F, 256), bf),
            pltpu.VMEM((4, 2 * F, 128), bf),
            pltpu.VMEM((width, 128), bf),
            pltpu.VMEM((a_count, j_count, width), bf),
            pltpu.VMEM((nr, 128, width), bf),
            pltpu.VMEM((tile_rows // 128, 128), fl),
            pltpu.VMEM((tile_rows // 256, 128), fl),
            pltpu.VMEM((chips, tile_rows // 256, 128), fl),
            dma((4,)), dma((5,)), dma((5,)), dma, dma, dma, dma, dma((nc,)), dma, dma,
            dma, dma, dma, dma, dma, dma((nr,)), dma((nr,)), dma, dma,
        ],
        compiler_params=pltpu.CompilerParams(
            collective_id=0, has_side_effects=True, vmem_limit_bytes=48 * 1024 * 1024),
    )(embeddings.T, assigned.reshape(lines, 128), centroids)
    return out, best.reshape(rows)


def solution(mesh):
    nx, nz = mesh.shape["row"] // 2, mesh.shape["cent"] // 4
    return jax.shard_map(
        functools.partial(per_device, nx, nz),
        mesh=mesh,
        in_specs=(P("row", "cent"), P("row"), P("cent", None)),
        out_specs=(P("cent", None), P("row")),
        check_vma=False,
    )
```

time: 111 us -> 91.7 us (0.83)
  Pallas kernels: 106 us -> 86.6 us
    pallas_call x1, Pallas kernels: 106 us -> 86.6 us  [per_device(): pl.pallas_call(functools.partial(kernel, nx, nz), out_shape=(jax.ShapeDty...]
where the time goes in v2:
time: 91.7 us; the launch traced here: 91.5 us
  Pallas kernels  86.6 us (94%)
  local copies, waits for them, and re-layouts  4.25 us (5%)
    pallas_call x1, Pallas kernels, per_device(): pl.pallas_call(functools.partial(kernel, nx, nz), out_shape=(jax.ShapeDty...  86.6 us
    unnamed x8, local copies, waits for them, and re-layouts  4.25 us

profile of v2, /device:TPU:1, one launch (start us, length us, event | category | flops | bytes accessed | tf_op | source)
XLA Modules:
  0.0 91.5 jit_solution(337046688309838988)
XLA Ops:
  0.6 0.0 copy-start
  0.6 1.0 %copy-done = bf16[8192,32]{0,1:T(8,128)(2,1)S(1)} copy-done((bf16[8192,32]{0,1:T(8,128)(2,1)S(1)}, bf16[8192,32]{0,1:T(8,128)(2,1)}, u32[]{:S(2)}) %copy-start) | copy-done | bytes 524312
  1.7 0.0 copy-start.1
  1.7 1.0 %copy-done.1 = bf16[256,1024]{1,0:T(8,128)(2,1)S(1)} copy-done((bf16[256,1024]{1,0:T(8,128)(2,1)S(1)}, bf16[256,1024]{1,0:T(8,128)(2,1)}, u32[]{:S(2)}) %copy-start.1) | copy-done | bytes 524312
  2.7 0.0 copy-start.2
  2.7 0.8 copy-done.2
  3.5 86.6 %shard_map.50 = (bf16[256,1024]{1,0:T(8,128)(2,1)S(1)}, f32[64,128]{1,0:T(8,128)S(1)}) custom-call(bf16[32,8192]{1,0:T(8,128)(2,1)S(1)} %bitcast.3, s32[64,128]{1,0:T(8,128)S(1)} %bitcast.4, bf16[256,1024]{1,0:T(8,128)(2,1)S(1)} %copy-done.1), custom_call_target="tpu_custom_call" | custom-call | tf_op jit(solution)/shard_map/pallas_call | solution.py:324
  90.0 0.8 copy.7
  90.8 0.6 copy.8
Async XLA Ops:
  0.6 1.0 %copy-start = (bf16[8192,32]{0,1:T(8,128)(2,1)S(1)}, bf16[8192,32]{0,1:T(8,128)(2,1)}, u32[]{:S(2)}) copy-start(bf16[8192,32]{0,1:T(8,128)(2,1)} %param.3) | copy-start | bytes 1572868
  1.7 1.0 %copy-start.1 = (bf16[256,1024]{1,0:T(8,128)(2,1)S(1)}, bf16[256,1024]{1,0:T(8,128)(2,1)}, u32[]{:S(2)}) copy-start(bf16[256,1024]{1,0:T(8,128)(2,1)} %cent_hbm.1) | copy-start | bytes 1572868
  2.7 0.8 copy-start.2

commit v3 on v2

--- a/solution.py
+++ b/solution.py
@@ -10,13 +10,15 @@
 MESH = pl.DeviceIdType.MESH
 F = 32
 EPS = 1e-06
-CUT = 48
+FIRST = 6
+CUT = 64
+TILE = 1024
 
 
 def kernel(nx, nz, x_hbm, id_ref, cent_hbm, nc_out, best_out,
            x_ref, q, qmate, qchip, inv, lanes, lows, e, kr, acc, part, got, summed, zb, turned, centbuf, ncs,
            top, topmate, tops, loc, m_send, m_recv, n_send, n_recv, ez_send, ef_send, e_recv, c_send, c_recv,
-           p_send, p_recv, s_send, s_recv, g_send, ga_recv, gb_recv, t_send, t_recv):
+           p_send, p_recv, s_send, s_recv, g_send, g_recv, t_send, t_recv):
     nr = 2 * nx
     nc = 4 * nz
     chips = 2 * nz
@@ -99,14 +101,17 @@
         d = lax.rem(chip + i, chips) * 2 + core
         remote(qchip.at[chip], qchip.at[chip], n_send, n_recv, r, d).start()
 
-    def turned_z(i):
-        return lax.rem(z + (i + 1) // 2 * (2 * lax.rem(i, 2) - 1) + nz, nz)
-
-    @pl.loop(1, nz)
-    def _(i):
-        zz = turned_z(i)
-        remote(x_ref.at[:, span((zz // 2) * tile_rows, tile_rows)], e.at[c], ez_send, e_recv.at[c],
-               r, cent_id(y, zz, core)).start()
+    outward = 2 * lax.rem(z, 2) - 1
+
+    def at_z(steps):
+        return lax.rem(z + outward * steps + nz, nz)
+
+    z_mate = cent_id(y, at_z(-1), core)
+    direct = (1, 2, 3) if nz == 8 else ()
+    for steps in (-1, 1, -2, 3) if nz == 8 else (-1,):
+        to = at_z(steps)
+        remote(x_ref.at[:, span((to // 2) * tile_rows, tile_rows)], e.at[c], ez_send, e_recv.at[c],
+               r, cent_id(y, to, core)).start()
 
     own_c.wait()
 
@@ -114,23 +119,27 @@
     def _(i):
         remote(centbuf.at[a], centbuf.at[a], c_send, c_recv, r, cent_id(y, lax.rem(z + 2 * i, nz), core)).start()
 
-    def pass_on(piece, to_y):
+    def pass_on(piece, to_z, to_y):
+        if to_z:
+            remote(e.at[piece], e.at[piece], ef_send, e_recv.at[piece], r, z_mate).start()
         if to_y:
             remote(e.at[piece], e.at[piece], ef_send, e_recv.at[piece], r, y_mate).start()
         remote(e.at[piece], e.at[piece], ef_send, e_recv.at[piece], r, core_mate).start()
 
-    def pass_z(i):
-        piece = cent_id(y, turned_z(i), core)
+    def pass_z(steps):
+        piece = cent_id(y, at_z(steps), core)
         drain(e.at[piece], e_recv.at[piece])
-        pass_on(piece, True)
-
-    def pass_y(i):
-        piece = cent_id(1 - y, lax.rem(z + i, nz), core)
+        pass_on(piece, steps > 0, True)
+
+    def pass_y(steps):
+        piece = cent_id(1 - y, at_z(steps), core)
         drain(e.at[piece], e_recv.at[piece])
-        pass_on(piece, False)
+        pass_on(piece, False, False)
+
+    order = (0, -1, 1, -2, 2, 3, -3, -4) if nz == 8 else (0, -1)
 
     own_e.wait()
-    pass_on(c, True)
+    pass_on(c, False, True)
 
     drain(qchip.at[pl.ds(0, chips - 1)], n_recv)
     squares = qchip[0].astype(jnp.float32)
@@ -172,11 +181,8 @@
 
     got[r] = part[span(r * 128, 128), :]
 
-    first_pass = 3 * nz // 4 + 1
-
-    @pl.loop(1, first_pass)
-    def _(i):
-        pass_z(i)
+    for steps in order[1:FIRST]:
+        pass_z(steps)
 
     drain(got.at[pl.ds(0, nr - 1)], p_recv)
     total = got[0].astype(jnp.float32)
@@ -200,82 +206,114 @@
     if a_count > 1:
         drain(centbuf.at[pl.ds(0, a_count - 1)], c_recv)
 
-    @pl.loop(first_pass, nz)
-    def _(i):
-        pass_z(i)
+    for steps in order[FIRST:]:
+        pass_z(steps)
+
+    for steps in order[:nz // 2]:
+        pass_y(steps)
 
     drain(turned.at[pl.ds(0, (chips - 1) * 2 * F), :], s_recv)
     fresh = turned[...].astype(jnp.float32).T + centbuf[...].reshape(128, width).astype(jnp.float32)
     fresh = fresh * lax.rsqrt(jnp.sum(fresh * fresh, axis=1, keepdims=True) + EPS)
-    ncs[r] = fresh.astype(jnp.bfloat16)
-
-    def pa(slot):
-        return ncs.at[slot, pl.ds(0, CUT), :]
-
-    def pb(slot):
-        return ncs.at[slot, pl.ds(CUT, 128 - CUT), :]
-
-    other = (1 - yh) * nx + x
-    remote(pa(r), pa(r), g_send, ga_recv.at[r], other, c).start()
-    for i in range(1, nx):
-        mate = yh * nx + lax.rem(x + i, nx)
-        remote(pb(r), pb(r), g_send, gb_recv.at[r], mate, c).start()
-    for i in range(1, nx):
-        mate = yh * nx + lax.rem(x + i, nx)
-        remote(pa(r), pa(r), g_send, ga_recv.at[r], mate, c).start()
-    remote(pb(r), pb(r), g_send, gb_recv.at[r], other, c).start()
-    drain(pa(other), ga_recv.at[other])
-    for i in range(1, nx):
-        mate = yh * nx + lax.rem(x + i, nx)
-        remote(pa(other), pa(other), g_send, ga_recv.at[other], mate, c).start()
-    for i in range(1, nx):
-        near = yh * nx + lax.rem(x + i, nx)
-        drain(pb(near), gb_recv.at[near])
-        remote(pb(near), pb(near), g_send, gb_recv.at[near], other, c).start()
-
-    @pl.loop(0, nz)
-    def _(i):
-        pass_y(i)
+    ncs[0] = fresh.astype(jnp.bfloat16)
+
+    up = yh * nx + lax.rem(x + 1, nx)
+    down = yh * nx + lax.rem(x + nx - 1, nx)
+    over = (1 - yh) * nx + x
+
+    def cut(part, side):
+        first, size = ((0, CUT), (CUT, 128 - CUT))[part]
+        if side is None:
+            return pl.ds(first, size)
+        return pl.ds(first + side * (size // 2), size // 2)
+
+    def push(slot, to, part, side, target):
+        kind = part * 3 + (0 if side is None else 1 + side)
+        rows_of = cut(part, side)
+        remote(ncs.at[slot, rows_of, :], ncs.at[to, rows_of, :], g_send, g_recv.at[to, kind], target, c).start()
+
+    def arrive(slot, part, side):
+        kind = part * 3 + (0 if side is None else 1 + side)
+        ref = ncs.at[slot, cut(part, side), :]
+        drain(ref, g_recv.at[slot, kind])
+
+    ring = nx == 4
+
+    def round_x(base, part):
+        push(base, base + nx - 1, part, None, up)
+        if ring:
+            push(base, base + 1, part, None, down)
+
+    def relay(base, part, also):
+        arrive(base + nx - 1, part, None)
+        if ring:
+            push(base + 3, base + 2, part, 0, up)
+        if also:
+            push(base + nx - 1, nx + base + nx - 1, part, None, over)
+        if ring:
+            arrive(base + 1, part, None)
+            push(base + 1, base + 2, part, 1, down)
+            if also:
+                push(base + 1, nx + base + 1, part, None, over)
+
+    push(0, nx, 0, None, over)
+    round_x(0, 1)
+    round_x(0, 0)
+    push(0, nx, 1, None, over)
+    relay(0, 1, True)
+    arrive(nx, 0, None)
+    round_x(nx, 0)
+    relay(0, 0, False)
+    if ring:
+        for side in range(2):
+            arrive(2, 1, side)
+            push(2, nx + 2, 1, side, over)
+
+    for steps in order[nz // 2:]:
+        pass_y(steps)
+
+    relay(nx, 0, False)
 
     @pl.loop(0, 2 * nz)
     def _(i):
         piece = cent_id(i // nz, lax.rem(i, nz), 1 - core)
         drain(e.at[piece], e_recv.at[piece])
 
-    for i in range(1, nx):
-        near = yh * nx + lax.rem(x + i, nx)
-        drain(pa(near), ga_recv.at[near])
-
-    wide_rows = 256
-
-    def score(first_slot, merge):
-        block = ncs[pl.ds(first_slot, nx)].reshape(nx * 128, width)
-
-        @pl.loop(0, tile_rows // wide_rows)
+    if ring:
+        for side in range(2):
+            arrive(2, 0, side)
+    arrive(nx, 1, None)
+
+    def score(first_slot, slots, merge):
+        block = ncs[first_slot:first_slot + slots].reshape(slots * 128, width)
+
+        @pl.loop(0, tile_rows // TILE)
         def _(t):
-            here = span(t * wide_rows, wide_rows)
-            scores = jnp.dot(block, e[:, :, here].reshape(width, wide_rows), preferred_element_type=jnp.float32)
+            here = span(t * TILE, TILE)
+            scores = jnp.dot(block, e[:, :, here].reshape(width, TILE), preferred_element_type=jnp.float32)
             best = jnp.max(scores, axis=0, keepdims=True)
-            for k in range(2):
-                line = pl.ds(t * 2 + k, 1)
+            for k in range(TILE // 128):
+                line = pl.ds(t * (TILE // 128) + k, 1)
                 piece = best[:, k * 128:(k + 1) * 128]
                 top[line, :] = jnp.maximum(top[line, :], piece) if merge else piece
 
-    score(yh * nx, False)
-
-    for i in range(1, nx):
-        far = (1 - yh) * nx + lax.rem(x + i, nx)
-        drain(pa(far), ga_recv.at[far])
-        drain(pb(far), gb_recv.at[far])
-    drain(pb(other), gb_recv.at[other])
-
-    score((1 - yh) * nx, True)
+    score(0, nx + 1, False)
+
+    arrive(nx + nx - 1, 1, None)
+    if ring:
+        arrive(nx + 1, 1, None)
+        for side in range(2):
+            arrive(nx + 2, 0, side)
+            arrive(nx + 2, 1, side)
+
+    score(nx + 1, nx - 1, True)
 
     own_half = tile_lines // 2
     swap_t = remote(top.at[span((1 - core) * own_half, own_half), :], topmate, m_send.at[3], m_recv.at[3], r, core_mate)
     swap_t.start()
     for i in range(nr):
-        nc_out[i * j_count:(i + 1) * j_count, :] = ncs[i, span(a * j_count, j_count), :]
+        row = (yh if i < nx else 1 - yh) * nx + lax.rem(x + i, nx)
+        nc_out[span(row * j_count, j_count), :] = ncs[i, span(a * j_count, j_count), :]
     swap_t.wait()
     tops[chip] = jnp.maximum(top[span(core * own_half, own_half), :], topmate[...])
 
@@ -285,8 +323,8 @@
         remote(tops.at[chip], tops.at[chip], t_send, t_recv, r, d).start()
 
     drain(qchip.at[pl.ds(0, chips - 1)], n_send)
-    drain(e.at[pl.ds(0, nz - 1)], ez_send)
-    drain(e.at[pl.ds(0, 3 * nz)], ef_send)
+    drain(e.at[pl.ds(0, 1 + len(direct))], ez_send)
+    drain(e.at[pl.ds(0, 3 * nz + len(direct))], ef_send)
     if a_count > 1:
         drain(centbuf.at[pl.ds(0, a_count - 1)], c_send)
     drain(got.at[pl.ds(0, nr - 1)], p_send)
@@ -348,7 +386,7 @@
             pltpu.VMEM((tile_rows // 256, 128), fl),
             pltpu.VMEM((chips, tile_rows // 256, 128), fl),
             dma((4,)), dma((5,)), dma((5,)), dma, dma, dma, dma, dma((nc,)), dma, dma,
-            dma, dma, dma, dma, dma, dma((nr,)), dma((nr,)), dma, dma,
+            dma, dma, dma, dma, dma, dma((nr, 6)), dma, dma,
         ],
         compiler_params=pltpu.CompilerParams(
             collective_id=0, has_side_effects=True, vmem_limit_bytes=48 * 1024 * 1024),

time: 91.7 us -> 86.4 us (0.942)
  Pallas kernels: 86.6 us -> 81.3 us
    pallas_call x1, Pallas kernels: 86.6 us -> 81.3 us  [per_device(): pl.pallas_call(functools.partial(kernel, nx, nz), out_shape=(jax.ShapeDty...]
where the time goes in v3:
time: 86.4 us; the launch traced here: 86.2 us
  Pallas kernels  81.3 us (94%)
  local copies, waits for them, and re-layouts  4.25 us (5%)
    pallas_call x1, Pallas kernels, per_device(): pl.pallas_call(functools.partial(kernel, nx, nz), out_shape=(jax.ShapeDty...  81.3 us
    unnamed x8, local copies, waits for them, and re-layouts  4.25 us

profile of v3, /device:TPU:1, one launch (start us, length us, event | category | flops | bytes accessed | tf_op | source)
XLA Modules:
  0.0 86.2 jit_solution(7508128636952264591)
XLA Ops:
  0.6 0.0 copy-start
  0.6 1.0 %copy-done = bf16[8192,32]{0,1:T(8,128)(2,1)S(1)} copy-done((bf16[8192,32]{0,1:T(8,128)(2,1)S(1)}, bf16[8192,32]{0,1:T(8,128)(2,1)}, u32[]{:S(2)}) %copy-start) | copy-done | bytes 524312
  1.7 0.0 copy-start.1
  1.7 1.0 %copy-done.1 = bf16[256,1024]{1,0:T(8,128)(2,1)S(1)} copy-done((bf16[256,1024]{1,0:T(8,128)(2,1)S(1)}, bf16[256,1024]{1,0:T(8,128)(2,1)}, u32[]{:S(2)}) %copy-start.1) | copy-done | bytes 524312
  2.7 0.0 copy-start.2
  2.7 0.8 copy-done.2
  3.5 81.3 %shard_map.50 = (bf16[256,1024]{1,0:T(8,128)(2,1)S(1)}, f32[64,128]{1,0:T(8,128)S(1)}) custom-call(bf16[32,8192]{1,0:T(8,128)(2,1)S(1)} %bitcast.3, s32[64,128]{1,0:T(8,128)S(1)} %bitcast.4, bf16[256,1024]{1,0:T(8,128)(2,1)S(1)} %copy-done.1), custom_call_target="tpu_custom_call" | custom-call | tf_op jit(solution)/shard_map/pallas_call | solution.py:362
  84.8 0.8 copy.7
  85.6 0.6 copy.8
Async XLA Ops:
  0.6 1.0 %copy-start = (bf16[8192,32]{0,1:T(8,128)(2,1)S(1)}, bf16[8192,32]{0,1:T(8,128)(2,1)}, u32[]{:S(2)}) copy-start(bf16[8192,32]{0,1:T(8,128)(2,1)} %param.3) | copy-start | bytes 1572868
  1.7 1.0 %copy-start.1 = (bf16[256,1024]{1,0:T(8,128)(2,1)S(1)}, bf16[256,1024]{1,0:T(8,128)(2,1)}, u32[]{:S(2)}) copy-start(bf16[256,1024]{1,0:T(8,128)(2,1)} %cent_hbm.1) | copy-start | bytes 1572868
  2.7 0.8 copy-start.2

commit v4 on v3

--- a/solution.py
+++ b/solution.py
@@ -10,13 +10,12 @@
 MESH = pl.DeviceIdType.MESH
 F = 32
 EPS = 1e-06
-FIRST = 6
 CUT = 64
 TILE = 1024
 
 
 def kernel(nx, nz, x_hbm, id_ref, cent_hbm, nc_out, best_out,
-           x_ref, q, qmate, qchip, inv, lanes, lows, e, kr, acc, part, got, summed, zb, turned, centbuf, ncs,
+           x_ref, q, qmate, qchip, inv, lanes, lows, hot, unit, e, kr, acc, part, got, summed, zb, turned, centbuf, ncs,
            top, topmate, tops, loc, m_send, m_recv, n_send, n_recv, ez_send, ef_send, e_recv, c_send, c_recv,
            p_send, p_recv, s_send, s_recv, g_send, g_recv, t_send, t_recv):
     nr = 2 * nx
@@ -77,7 +76,8 @@
     cc = ids // (nr * j_count)
     zz = lax.rem(cc // 2, nz)
     lanes[...] = (lax.rem(cc, 2) * 128 + (zz // 2) * j_count + lax.rem(ids, j_count)).astype(jnp.float32)
-    lows[...] = (lax.rem(ids, nr * j_count) // j_count * 4 + (cc // (2 * nz)) * 2 + lax.rem(zz, 2)).astype(jnp.float32)
+    ahead = lax.rem(lax.rem(ids, nr * j_count) // j_count + (2 * nr - 1) - r, nr)
+    lows[...] = (ahead * 4 + (cc // (2 * nz)) * 2 + lax.rem(zz, 2)).astype(jnp.float32)
 
     in_x.wait()
 
@@ -129,17 +129,26 @@
     def pass_z(steps):
         piece = cent_id(y, at_z(steps), core)
         drain(e.at[piece], e_recv.at[piece])
-        pass_on(piece, steps > 0, True)
+        pass_on(piece, steps > 0, steps > 0)
 
     def pass_y(steps):
         piece = cent_id(1 - y, at_z(steps), core)
         drain(e.at[piece], e_recv.at[piece])
-        pass_on(piece, False, False)
-
-    order = (0, -1, 1, -2, 2, 3, -3, -4) if nz == 8 else (0, -1)
+        pass_on(piece, steps >= 0, False)
+
+    near, far = ((0, 1, 2, 3), (-1, -2, -3, -4)) if nz == 8 else ((0,), (-1,))
 
     own_e.wait()
     pass_on(c, False, True)
+
+    def along(block):
+        return jnp.concatenate([block[k:k + 1, :] for k in range(8)], axis=1)
+
+    @pl.loop(0, lines // 8)
+    def _(t):
+        lane_b = jnp.broadcast_to(along(lanes[span(t * 8, 8), :]), (256, 1024)).astype(jnp.bfloat16)
+        iota = lax.broadcasted_iota(jnp.int32, (256, 1024), 0).astype(jnp.float32).astype(jnp.bfloat16)
+        hot[:, span(t * 1024, 1024)] = jnp.where(lane_b == iota, jnp.bfloat16(1), jnp.bfloat16(0))
 
     drain(qchip.at[pl.ds(0, chips - 1)], n_recv)
     squares = qchip[0].astype(jnp.float32)
@@ -151,37 +160,41 @@
     swap_i.start()
     swap_i.wait()
 
-    acc[...] = jnp.zeros_like(acc)
-    klo_count = 4 * nr
-
-    def along(block):
-        return jnp.concatenate([block[k:k + 1, :] for k in range(8)], axis=1)
+    group = nr // 2
+    block_rows = 4 * F
 
     @pl.loop(0, lines // 8)
     def _(t):
-        own8 = span(t * 8, 8)
-        scale = along(inv[own8, :])
-        unit = (x_ref[:, span(t * 1024, 1024)].astype(jnp.float32) * scale).astype(jnp.bfloat16)
-        lane_b = jnp.broadcast_to(along(lanes[own8, :]), (256, 1024)).astype(jnp.bfloat16)
-        iota = lax.broadcasted_iota(jnp.int32, (256, 1024), 0).astype(jnp.float32).astype(jnp.bfloat16)
-        one = jnp.bfloat16(1)
-        nil = jnp.bfloat16(0)
-        hot = jnp.where(lane_b == iota, one, nil)
-        low_b = jnp.broadcast_to(along(lows[own8, :]), (F, 1024)).astype(jnp.bfloat16)
-        for j in range(klo_count):
-            kr[j * F:(j + 1) * F, :] = jnp.where(low_b == jnp.bfloat16(j), unit, nil)
-        acc[...] += lax.dot_general(kr[...], hot, (((1,), (1,)), ((), ())), preferred_element_type=jnp.float32)
-
-    part[...] = acc[...].astype(jnp.bfloat16)
-
-    @pl.loop(1, nr)
-    def _(i):
-        rr = lax.rem(r + i, nr)
-        remote(part.at[span(rr * 128, 128), :], got.at[r], p_send, p_recv, rr, c).start()
-
-    got[r] = part[span(r * 128, 128), :]
-
-    for steps in order[1:FIRST]:
+        here = span(t * 1024, 1024)
+        unit[:, here] = (x_ref[:, here].astype(jnp.float32) * along(inv[span(t * 8, 8), :])).astype(jnp.bfloat16)
+
+    for g in range(2):
+        @pl.loop(0, lines // 8)
+        def _(t):
+            here = span(t * 1024, 1024)
+            low_b = jnp.broadcast_to(along(lows[span(t * 8, 8), :]), (F, 1024)).astype(jnp.bfloat16)
+            mine = unit[:, here]
+            for j in range(4 * group):
+                kr[j * F:(j + 1) * F, :] = jnp.where(low_b == jnp.bfloat16(g * 4 * group + j), mine, jnp.bfloat16(0))
+            product = lax.dot_general(kr[...], hot[:, here], (((1,), (1,)), ((), ())), preferred_element_type=jnp.float32)
+
+            @pl.when(t == 0)
+            def _():
+                acc[...] = product
+
+            @pl.when(t > 0)
+            def _():
+                acc[...] += product
+
+        part[g * group * block_rows:(g + 1) * group * block_rows, :] = acc[...].astype(jnp.bfloat16)
+        for k in range(g * group, (g + 1) * group):
+            if k < nr - 1:
+                remote(part.at[pl.ds(k * block_rows, block_rows), :], got.at[r], p_send, p_recv,
+                       lax.rem(r + 1 + k, nr), c).start()
+
+    got[r] = part[(nr - 1) * block_rows:, :]
+
+    for steps in near[1:]:
         pass_z(steps)
 
     drain(got.at[pl.ds(0, nr - 1)], p_recv)
@@ -206,10 +219,10 @@
     if a_count > 1:
         drain(centbuf.at[pl.ds(0, a_count - 1)], c_recv)
 
-    for steps in order[FIRST:]:
+    for steps in far:
         pass_z(steps)
 
-    for steps in order[:nz // 2]:
+    for steps in near:
         pass_y(steps)
 
     drain(turned.at[pl.ds(0, (chips - 1) * 2 * F), :], s_recv)
@@ -269,7 +282,7 @@
             arrive(2, 1, side)
             push(2, nx + 2, 1, side, over)
 
-    for steps in order[nz // 2:]:
+    for steps in far:
         pass_y(steps)
 
     relay(nx, 0, False)
@@ -313,7 +326,8 @@
     swap_t.start()
     for i in range(nr):
         row = (yh if i < nx else 1 - yh) * nx + lax.rem(x + i, nx)
-        nc_out[span(row * j_count, j_count), :] = ncs[i, span(a * j_count, j_count), :]
+        pltpu.make_async_copy(ncs.at[i, span(a * j_count, j_count), :], nc_out.at[span(row * j_count, j_count), :],
+                              loc.at[3]).start()
     swap_t.wait()
     tops[chip] = jnp.maximum(top[span(core * own_half, own_half), :], topmate[...])
 
@@ -324,7 +338,7 @@
 
     drain(qchip.at[pl.ds(0, chips - 1)], n_send)
     drain(e.at[pl.ds(0, 1 + len(direct))], ez_send)
-    drain(e.at[pl.ds(0, 3 * nz + len(direct))], ef_send)
+    drain(e.at[pl.ds(0, 2 + 3 * len(direct) + len(far) * 2 + len(near) * 2)], ef_send)
     if a_count > 1:
         drain(centbuf.at[pl.ds(0, a_count - 1)], c_send)
     drain(got.at[pl.ds(0, nr - 1)], p_send)
@@ -345,6 +359,7 @@
     drain(best_out.at[pl.ds(0, half), :], m_recv.at[4])
     drain(best_out.at[pl.ds(0, half), :], m_send.at[4])
     drain(tops.at[pl.ds(0, chips - 1)], t_send)
+    drain(nc_out, loc.at[3])
 
 
 def per_device(nx, nz, embeddings, assigned, centroids):
@@ -363,7 +378,7 @@
         functools.partial(kernel, nx, nz),
         out_shape=(jax.ShapeDtypeStruct((owned, width), bf), jax.ShapeDtypeStruct((lines, 128), fl)),
         in_specs=[hbm, vmem, hbm],
-        out_specs=(vmem, vmem),
+        out_specs=(hbm, vmem),
         scratch_shapes=[
             pltpu.VMEM((F, rows), bf),
             pltpu.VMEM((lines, 128), fl),
@@ -372,9 +387,11 @@
             pltpu.VMEM((lines, 128), fl),
             pltpu.VMEM((lines, 128), fl),
             pltpu.VMEM((lines, 128), fl),
+            pltpu.VMEM((256, rows), bf),
+            pltpu.VMEM((F, rows), bf),
             pltpu.VMEM((nc, F, tile_rows), bf),
-            pltpu.VMEM((4 * nr * F, 1024), bf),
-            pltpu.VMEM((4 * nr * F, 256), fl),
+            pltpu.VMEM((2 * nr * F, 1024), bf),
+            pltpu.VMEM((2 * nr * F, 256), fl),
             pltpu.VMEM((4 * nr * F, 256), bf),
             pltpu.VMEM((nr, 128, 256), bf),
             pltpu.VMEM((4, F, 256), bf),
@@ -389,7 +406,7 @@
             dma, dma, dma, dma, dma, dma((nr, 6)), dma, dma,
         ],
         compiler_params=pltpu.CompilerParams(
-            collective_id=0, has_side_effects=True, vmem_limit_bytes=48 * 1024 * 1024),
+            collective_id=0, has_side_effects=True, vmem_limit_bytes=58 * 1024 * 1024),
     )(embeddings.T, assigned.reshape(lines, 128), centroids)
     return out, best.reshape(rows)
 

time: 86.4 us -> 81.7 us (0.946)
  Pallas kernels: 81.3 us -> 78.3 us
  local copies, waits for them, and re-layouts: 4.25 us -> 2.5 us
    pallas_call x1, Pallas kernels: 81.3 us -> 78.3 us  [per_device(): pl.pallas_call(functools.partial(kernel, nx, nz), out_shape=(jax.ShapeDty...]
    unnamed x8 -> x4, local copies, waits for them, and re-layouts: 4.25 us -> 2.5 us
where the time goes in v4:
time: 81.7 us; the launch traced here: 81.5 us
  Pallas kernels  78.3 us (96%)
  local copies, waits for them, and re-layouts  2.5 us (3%)
    pallas_call x1, Pallas kernels, per_device(): pl.pallas_call(functools.partial(kernel, nx, nz), out_shape=(jax.ShapeDty...  78.3 us
    unnamed x4, local copies, waits for them, and re-layouts  2.5 us

profile of v4, /device:TPU:1, one launch (start us, length us, event | category | flops | bytes accessed | tf_op | source)
XLA Modules:
  0.0 81.5 jit_solution(12617457242223636304)
XLA Ops:
  0.6 78.3 %shard_map.50 = (bf16[256,1024]{1,0:T(8,128)(2,1)}, f32[64,128]{1,0:T(8,128)}) custom-call(bf16[32,8192]{1,0:T(8,128)(2,1)} %bitcast.3, s32[64,128]{1,0:T(8,128)} %bitcast.4, bf16[256,1024]{1,0:T(8,128)(2,1)} %cent_hbm.1), custom_call_target="tpu_custom_call" | custom-call | tf_op jit(solution)/shard_map/pallas_call | solution.py:377
  79.0 0.0 copy-start
  79.0 1.9 %copy.7 = bf16[256,1024]{1,0:T(8,128)(2,1)} copy(bf16[256,1024]{1,0:T(8,128)(2,1)} %get-tuple-element.8) | data formatting | bytes 1048576
  80.9 0.0 copy-done
  80.9 0.6 copy.8
Async XLA Ops:
  79.0 1.9 %copy-start = (f32[64,128]{1,0:T(8,128)S(1)}, f32[64,128]{1,0:T(8,128)}, u32[]{:S(2)}) copy-start(f32[64,128]{1,0:T(8,128)} %get-tuple-element.5) | copy-start | bytes 98308

commit v5 on v4

--- a/solution.py
+++ b/solution.py
@@ -10,12 +10,13 @@
 MESH = pl.DeviceIdType.MESH
 F = 32
 EPS = 1e-06
+CHUNK = 4096
 CUT = 64
 TILE = 1024
 
 
 def kernel(nx, nz, x_hbm, id_ref, cent_hbm, nc_out, best_out,
-           x_ref, q, qmate, qchip, inv, lanes, lows, hot, unit, e, kr, acc, part, got, summed, zb, turned, centbuf, ncs,
+           x_ref, q, qmate, qchip, inv, lanes, lows, hot, spread, e, acc, part, got, summed, zb, turned, centbuf, ncs,
            top, topmate, tops, loc, m_send, m_recv, n_send, n_recv, ez_send, ef_send, e_recv, c_send, c_recv,
            p_send, p_recv, s_send, s_recv, g_send, g_recv, t_send, t_recv):
     nr = 2 * nx
@@ -144,11 +145,22 @@
     def along(block):
         return jnp.concatenate([block[k:k + 1, :] for k in range(8)], axis=1)
 
+    def packed(block):
+        return jnp.broadcast_to(along(block), (16, 1024)).astype(jnp.bfloat16)
+
     @pl.loop(0, lines // 8)
     def _(t):
-        lane_b = jnp.broadcast_to(along(lanes[span(t * 8, 8), :]), (256, 1024)).astype(jnp.bfloat16)
-        iota = lax.broadcasted_iota(jnp.int32, (256, 1024), 0).astype(jnp.float32).astype(jnp.bfloat16)
-        hot[:, span(t * 1024, 1024)] = jnp.where(lane_b == iota, jnp.bfloat16(1), jnp.bfloat16(0))
+        here, lines8 = span(t * 1024, 1024), span(t * 8, 8)
+        lane_b, low_b = packed(lanes[lines8, :]), packed(lows[lines8, :])
+        iota = lax.broadcasted_iota(jnp.int32, (16, 1024), 0).astype(jnp.float32)
+        for k in range(16):
+            hot[k * 16:(k + 1) * 16, here] = jnp.where(
+                lane_b == (iota + k * 16).astype(jnp.bfloat16), jnp.bfloat16(1), jnp.bfloat16(0))
+        for k in range(F // 16):
+            mine = x_ref[k * 16:(k + 1) * 16, here]
+            for j in range(4 * nr):
+                at = j * F + k * 16
+                spread[at:at + 16, here] = jnp.where(low_b == jnp.bfloat16(j), mine, jnp.bfloat16(0))
 
     drain(qchip.at[pl.ds(0, chips - 1)], n_recv)
     squares = qchip[0].astype(jnp.float32)
@@ -166,17 +178,17 @@
     @pl.loop(0, lines // 8)
     def _(t):
         here = span(t * 1024, 1024)
-        unit[:, here] = (x_ref[:, here].astype(jnp.float32) * along(inv[span(t * 8, 8), :])).astype(jnp.bfloat16)
+        scale = packed(inv[span(t * 8, 8), :])
+        for k in range(16):
+            hot[k * 16:(k + 1) * 16, here] = hot[k * 16:(k + 1) * 16, here] * scale
 
     for g in range(2):
-        @pl.loop(0, lines // 8)
+        @pl.loop(0, rows // CHUNK)
         def _(t):
-            here = span(t * 1024, 1024)
-            low_b = jnp.broadcast_to(along(lows[span(t * 8, 8), :]), (F, 1024)).astype(jnp.bfloat16)
-            mine = unit[:, here]
-            for j in range(4 * group):
-                kr[j * F:(j + 1) * F, :] = jnp.where(low_b == jnp.bfloat16(g * 4 * group + j), mine, jnp.bfloat16(0))
-            product = lax.dot_general(kr[...], hot[:, here], (((1,), (1,)), ((), ())), preferred_element_type=jnp.float32)
+            here = span(t * CHUNK, CHUNK)
+            product = lax.dot_general(
+                spread[g * group * block_rows:(g + 1) * group * block_rows, here], hot[:, here],
+                (((1,), (1,)), ((), ())), preferred_element_type=jnp.float32)
 
             @pl.when(t == 0)
             def _():
@@ -388,9 +400,8 @@
             pltpu.VMEM((lines, 128), fl),
             pltpu.VMEM((lines, 128), fl),
             pltpu.VMEM((256, rows), bf),
-            pltpu.VMEM((F, rows), bf),
+            pltpu.VMEM((4 * nr * F, rows), bf),
             pltpu.VMEM((nc, F, tile_rows), bf),
-            pltpu.VMEM((2 * nr * F, 1024), bf),
             pltpu.VMEM((2 * nr * F, 256), fl),
             pltpu.VMEM((4 * nr * F, 256), bf),
             pltpu.VMEM((nr, 128, 256), bf),

time: 81.7 us -> 79.1 us (0.968)
  Pallas kernels: 78.3 us -> 75.8 us
    pallas_call x1, Pallas kernels: 78.3 us -> 75.8 us  [per_device(): pl.pallas_call(functools.partial(kernel, nx, nz), out_shape=(jax.ShapeDty...]
where the time goes in v5:
time: 79.1 us; the launch traced here: 78.9 us
  Pallas kernels  75.8 us (96%)
  local copies, waits for them, and re-layouts  2.5 us (3%)
    pallas_call x1, Pallas kernels, per_device(): pl.pallas_call(functools.partial(kernel, nx, nz), out_shape=(jax.ShapeDty...  75.8 us
    unnamed x4, local copies, waits for them, and re-layouts  2.5 us

profile of v5, /device:TPU:1, one launch (start us, length us, event | category | flops | bytes accessed | tf_op | source)
XLA Modules:
  0.0 78.9 jit_solution(6679460446643283224)
XLA Ops:
  0.6 75.8 %shard_map.50 = (bf16[256,1024]{1,0:T(8,128)(2,1)}, f32[64,128]{1,0:T(8,128)}) custom-call(bf16[32,8192]{1,0:T(8,128)(2,1)} %bitcast.3, s32[64,128]{1,0:T(8,128)} %bitcast.4, bf16[256,1024]{1,0:T(8,128)(2,1)} %cent_hbm.1), custom_call_target="tpu_custom_call" | custom-call | tf_op jit(solution)/shard_map/pallas_call | solution.py:389
  76.4 0.0 copy-start
  76.4 1.9 %copy.7 = bf16[256,1024]{1,0:T(8,128)(2,1)} copy(bf16[256,1024]{1,0:T(8,128)(2,1)} %get-tuple-element.8) | data formatting | bytes 1048576
  78.3 0.0 copy-done
  78.3 0.6 copy.8
Async XLA Ops:
  76.4 1.9 %copy-start = (f32[64,128]{1,0:T(8,128)S(1)}, f32[64,128]{1,0:T(8,128)}, u32[]{:S(2)}) copy-start(f32[64,128]{1,0:T(8,128)} %get-tuple-element.5) | copy-start | bytes 98308

commit v6 on v5

--- a/solution.py
+++ b/solution.py
@@ -12,7 +12,7 @@
 EPS = 1e-06
 CHUNK = 4096
 CUT = 64
-TILE = 1024
+TILE = 2048
 
 
 def kernel(nx, nz, x_hbm, id_ref, cent_hbm, nc_out, best_out,
@@ -130,12 +130,12 @@
     def pass_z(steps):
         piece = cent_id(y, at_z(steps), core)
         drain(e.at[piece], e_recv.at[piece])
-        pass_on(piece, steps > 0, steps > 0)
+        pass_on(piece, steps > 0, steps > 0 or steps in (-1, -2))
 
     def pass_y(steps):
         piece = cent_id(1 - y, at_z(steps), core)
         drain(e.at[piece], e_recv.at[piece])
-        pass_on(piece, steps >= 0, False)
+        pass_on(piece, steps in (2, 3), False)
 
     near, far = ((0, 1, 2, 3), (-1, -2, -3, -4)) if nz == 8 else ((0,), (-1,))
 
@@ -206,6 +206,7 @@
 
     got[r] = part[(nr - 1) * block_rows:, :]
 
+    pass_z(-1)
     for steps in near[1:]:
         pass_z(steps)
 
@@ -231,7 +232,7 @@
     if a_count > 1:
         drain(centbuf.at[pl.ds(0, a_count - 1)], c_recv)
 
-    for steps in far:
+    for steps in far[1:]:
         pass_z(steps)
 
     for steps in near:
@@ -281,8 +282,8 @@
             if also:
                 push(base + 1, nx + base + 1, part, None, over)
 
+    round_x(0, 1)
     push(0, nx, 0, None, over)
-    round_x(0, 1)
     round_x(0, 0)
     push(0, nx, 1, None, over)
     relay(0, 1, True)

time: 79.1 us -> 78.7 us (level)
  no operation moved by 1% of the time
where the time goes in v6:
time: 78.7 us; the launch traced here: 78.5 us
  Pallas kernels  75.3 us (96%)
  local copies, waits for them, and re-layouts  2.5 us (3%)
    pallas_call x1, Pallas kernels, per_device(): pl.pallas_call(functools.partial(kernel, nx, nz), out_shape=(jax.ShapeDty...  75.3 us
    unnamed x4, local copies, waits for them, and re-layouts  2.5 us

profile of v6, /device:TPU:1, one launch (start us, length us, event | category | flops | bytes accessed | tf_op | source)
XLA Modules:
  0.0 78.5 jit_solution(12457095523669869481)
XLA Ops:
  0.6 75.3 %shard_map.50 = (bf16[256,1024]{1,0:T(8,128)(2,1)}, f32[64,128]{1,0:T(8,128)}) custom-call(bf16[32,8192]{1,0:T(8,128)(2,1)} %bitcast.3, s32[64,128]{1,0:T(8,128)} %bitcast.4, bf16[256,1024]{1,0:T(8,128)(2,1)} %cent_hbm.1), custom_call_target="tpu_custom_call" | custom-call | tf_op jit(solution)/shard_map/pallas_call | solution.py:390
  76.0 0.0 copy-start
  76.0 1.9 %copy.7 = bf16[256,1024]{1,0:T(8,128)(2,1)} copy(bf16[256,1024]{1,0:T(8,128)(2,1)} %get-tuple-element.8) | data formatting | bytes 1048576
  77.9 0.0 copy-done
  77.9 0.6 copy.8
Async XLA Ops:
  76.0 1.9 %copy-start = (f32[64,128]{1,0:T(8,128)S(1)}, f32[64,128]{1,0:T(8,128)}, u32[]{:S(2)}) copy-start(f32[64,128]{1,0:T(8,128)} %get-tuple-element.5) | copy-start | bytes 98308
